TPU v7x, 128 devices: a whole 4x4x4 slice. The times are simulated.
128 devices in a mesh: wide: 32 (over y, x, z_hi), blk: 4 (over z_lo, core).
Axes of the slice: x: 4, y: 4, z: 4 (z_hi: 2, z_lo: 2; z = z_hi * 2 + z_lo), core: 2. Of those that a mesh axis runs over, the one named last changes fastest.
Arguments:
- visual_features: bfloat16 [131072, 1152], P(('wide', 'blk')), may hold values from -0.1875 to 0.1875
- sentence_features: bfloat16 [4096, 1152], P(('wide', 'blk')), may hold values from -0.1875 to 0.1875
- true_partner_ids: int32 [131072], P(('wide', 'blk')), may hold values from 0 to 4095
- inverse_warmth: float32 [], replicated, may hold values from 90 to 110
- additive_adjust: float32 [], replicated, may hold values from -12 to -9
Outputs:
- grad_images: float32 [131072, 1152], P(('wide', 'blk'))
- grad_texts: float32 [4096, 1152], P(('wide', 'blk'))
Inputs may be any that keep to these rules, and one draw needn't show every extreme that they name: Image i is paired with text true_partner_ids[i]; a text may be paired with several images or none.
All inputs are finite; a program needn't handle non-finite values.
Results may differ from a plain program's by a relative error of at most 0.007.
Values may be sent and summed in bfloat16 or wider, within the bound.
A program may use at most 64 MiB of HBM per device.

v0:
```python
import jax
import jax.numpy as jnp
from jax import lax
from jax.sharding import PartitionSpec as P

AXES = ("wide", "blk")


def shards(images, texts, partners, scale, bias):
    joined = lax.all_gather(texts, AXES, axis=0, tiled=True)
    scores = lax.dot_general(
        images, joined, (((1,), (1,)), ((), ())), preferred_element_type=jnp.float32
    )
    logits = scale * scores + bias
    columns = lax.iota(jnp.int32, joined.shape[0])
    sign = jnp.where(partners[:, None] == columns[None, :], 1.0, -1.0).astype(jnp.float32)
    weights = (-scale * sign * jax.nn.sigmoid(-sign * logits)).astype(jnp.bfloat16)
    grad_images = jnp.dot(weights, joined, preferred_element_type=jnp.float32)
    part = lax.dot_general(
        weights, images, (((0,), (0,)), ((), ())), preferred_element_type=jnp.float32
    )
    grad_texts = lax.psum_scatter(
        part.astype(jnp.bfloat16), AXES, scatter_dimension=0, tiled=True
    ).astype(jnp.float32)
    return (grad_images, grad_texts)


def solution(mesh):
    return jax.shard_map(
        shards,
        mesh=mesh,
        in_specs=(P(AXES, None), P(AXES, None), P(AXES), P(), P()),
        out_specs=(P(AXES, None), P(AXES, None)),
        check_vma=False,
    )
```

profile of v0, /device:TPU:0, one launch (start us, length us, event | category | flops | bytes accessed | tf_op | source)
XLA Modules:
  0.0 343.1 jit_solution(3602282821613848416)
XLA Ops:
  7.2 0.0 copy-start
  7.2 0.0 all-gather.2.cloned.1.call-start
  7.2 0.7 all-gather.2.cloned.1.call-update
  7.9 0.0 reduce-scatter.2.cloned.1.call-start
  9.3 75.2 %all-gather.2.cloned.1.call-done = bf16[4096,1152]{1,0:T(8,128)(2,1)} async-done(((bf16[32,1152]{1,0:T(8,128)(2,1)}), bf16[4096,1152]{1,0:T(8,128)(2,1)}) %all-gather.2.cloned.1.call-update) | async-done | bytes 9437200 | tf_op jit(solution)/shard_map/all_gather | solution.py:10
  84.4 0.0 copy-done
  84.4 19.9 %fusion.1 = bf16[1024,4096]{1,0:T(8,128)(2,1)} fusion(bf16[1024,1152]{1,0:T(8,128)(2,1)S(1)} %copy-done, bf16[4096,1152]{1,0:T(8,128)(2,1)} %all-gather.2.cloned.1.call-done, f32[]{:T(128)S(6)} %copy.8, f32[]{:T(128)S(6)} %copy.7, s32[1024]{0:T(1024)} %param.7, f32[]{:T(128)S(6)} %neg.9), kind=kOutput, calls=%fused_computation.3 | convolution fusion | flops 9714008064 | bytes 20189196 | tf_op jit(solution)/shard_map/dot_general | solution.py:11
  104.4 15.7 %convolution_convert_fusion = bf16[4096,1152]{1,0:T(8,128)(2,1)} fusion(bf16[1024,4096]{1,0:T(8,128)(2,1)} %fusion.1, bf16[1024,1152]{1,0:T(8,128)(2,1)S(1)} %copy-done), kind=kOutput, calls=%fused_computation.10 | convolution fusion | flops 9668395008 | bytes 20185088 | tf_op jit(solution)/shard_map/dot_general | solution.py:19
  120.0 0.0 reduce-scatter.2.cloned.1.call-update
  120.1 17.7 %fusion.7 = f32[1024,1152]{1,0:T(8,128)} fusion(bf16[1024,4096]{1,0:T(8,128)(2,1)} %fusion.1, bf16[4096,1152]{1,0:T(8,128)(2,1)} %all-gather.2.cloned.1.call-done), kind=kOutput, calls=%fused_computation.11 | convolution fusion | flops 9663676416 | bytes 22544384 | tf_op jit(solution)/shard_map/dot_general | solution.py:18
  137.8 197.0 %reduce-scatter.2.cloned.1.call-done = bf16[32,1152]{1,0:T(8,128)(2,1)} async-done(((bf16[4096,1152]{1,0:T(8,128)(2,1)}), bf16[32,1152]{1,0:T(8,128)(2,1)}) %reduce-scatter.2.cloned.1.call-update) | async-done | bytes 73744 | tf_op jit(solution)/shard_map/reduce_scatter | solution.py:22
  334.7 1.6 convert_element_type.11
Async XLA Ops:
  7.2 77.3 %copy-start = (bf16[1024,1152]{1,0:T(8,128)(2,1)S(1)}, bf16[1024,1152]{1,0:T(8,128)(2,1)}, u32[]{:S(2)}) copy-start(bf16[1024,1152]{1,0:T(8,128)(2,1)} %param.5) | copy-start | bytes 7077892
  7.2 77.2 %all-gather.2.cloned.1.call-start = ((), (), s32[]{:S(2)}) async-start(), calls=%async_computation.1 | async-start | bytes 9510912 | tf_op jit(solution)/shard_map/all_gather | solution.py:10
  7.9 326.8 %reduce-scatter.2.cloned.1.call-start = ((), (), s32[]{:S(2)}) async-start(), calls=%async_computation.2 | async-start | bytes 9510912 | tf_op jit(solution)/shard_map/reduce_scatter | solution.py:22
Sparse Core Ops, SparseCore 0:
  11.0 73.3 all-gather.1
  120.2 214.4 reduce-scatter.1
where the time goes:
time: 343 us
  waiting for transfers between devices  273 us (80%)
  matrix products  53.3 us (16%)
  between operations  15.3 us (4%)
    reduce_scatter x1, waiting for transfers between devices, shards(): lax.psum_scatter(part.astype(jnp.bfloat16), AXES, scatter_dimension=0, ti...  197 us
    all_gather x1, waiting for transfers between devices, shards(): joined = lax.all_gather(texts, AXES, axis=0, tiled=True)  75.2 us
    dot_general x1, matrix products, shards(): lax.dot_general(images, joined, (((1,), (1,)), ((), ())), preferred_eleme...  19.9 us
    dot_general x1, matrix products, shards(): grad_images = jnp.dot(weights, joined, preferred_element_type=jnp.float32)  17.7 us
    dot_general x1, matrix products, shards(): lax.dot_general(weights, images, (((0,), (0,)), ((), ())), preferred_elem...  15.7 us
  transfers between devices with their start and end apart: 2, of which 2 were waited for; matrix products, arithmetic and copies ran while one was open for 5% of the time, Pallas kernels for 0%

commit v1 on v0

--- a/solution.py
+++ b/solution.py
@@ -7,7 +7,9 @@
 
 
 def shards(images, texts, partners, scale, bias):
-    joined = lax.all_gather(texts, AXES, axis=0, tiled=True)
+    joined = jnp.concatenate(
+        lax.all_to_all(jnp.stack([texts] * lax.axis_size(AXES)), AXES, 0, 0), axis=0
+    )
     scores = lax.dot_general(
         images, joined, (((1,), (1,)), ((), ())), preferred_element_type=jnp.float32
     )

time: 343 us -> 403 us (1.17)
  waiting for transfers between devices: 273 us -> 315 us
  starting transfers between devices: 0.08 us -> 11.7 us
  local copies, waits for them, and re-layouts: 0.01 us -> 5.35 us
    all_to_all x0 -> x1, waiting for transfers between devices: none -> 113 us  [shards(): lax.all_to_all(jnp.stack([texts] * lax.axis_size(AXES)), AXES, 0, 0)]
    all_gather x1 -> x0, waiting for transfers between devices: 75.2 us -> none  [shards(): joined = lax.all_gather(texts, AXES, axis=0, tiled=True)]
    all_to_all x0 -> x1, starting transfers between devices: none -> 11.6 us  [shards(): lax.all_to_all(jnp.stack([texts] * lax.axis_size(AXES)), AXES, 0, 0)]
    another operation x0 -> x1, local copies, waits for them, and re-layouts: none -> 5.34 us  [shards(): jnp.stack([texts] * lax.axis_size(AXES))]
    reduce_scatter x1, waiting for transfers between devices: 197 us -> 202 us  [shards(): lax.psum_scatter(part.astype(jnp.bfloat16), AXES, scatter_dimension=0, ti...]
  transfers between devices with their start and end apart: 2 -> 2, of which waited for: 2 -> 2; matrix products, arithmetic and copies ran while one was open for 5% -> 4% of each run, Pallas kernels for 0% -> 0%
where the time goes in v1:
time: 403 us; the launch traced here: 402 us
  waiting for transfers between devices  315 us (78%)
  matrix products  53.3 us (13%)
  between operations  15.3 us (4%)
  starting transfers between devices  11.7 us (3%)
  local copies, waits for them, and re-layouts  5.35 us (1%)
    reduce_scatter x1, waiting for transfers between devices, shards(): lax.psum_scatter(part.astype(jnp.bfloat16), AXES, scatter_dimension=0, ti...  202 us
    all_to_all x1, waiting for transfers between devices, shards(): lax.all_to_all(jnp.stack([texts] * lax.axis_size(AXES)), AXES, 0, 0)  113 us
    dot_general x1, matrix products, shards(): lax.dot_general(images, joined, (((1,), (1,)), ((), ())), preferred_eleme...  19.9 us
    dot_general x1, matrix products, shards(): grad_images = jnp.dot(weights, joined, preferred_element_type=jnp.float32)  17.7 us
    dot_general x1, matrix products, shards(): lax.dot_general(weights, images, (((0,), (0,)), ((), ())), preferred_elem...  15.7 us
    all_to_all x1, starting transfers between devices, shards(): lax.all_to_all(jnp.stack([texts] * lax.axis_size(AXES)), AXES, 0, 0)  11.6 us
  transfers between devices with their start and end apart: 2, of which 2 were waited for; matrix products, arithmetic and copies ran while one was open for 4% of the time, Pallas kernels for 0%

profile of v1, /device:TPU:0, one launch (start us, length us, event | category | flops | bytes accessed | tf_op | source)
XLA Modules:
  0.0 402.3 jit_solution(3173724109755298490)
XLA Ops:
  7.2 0.0 copy-start
  7.2 5.3 %stack.2 = bf16[128,32,1152]{2,1,0:T(8,128)(2,1)} broadcast(bf16[32,1152]{1,0:T(8,128)(2,1)} %param.6), dimensions={1,2} | broadcast | bytes 9510912 | tf_op jit(solution)/shard_map/stack | solution.py:11
  12.5 0.0 copy-start.1
  12.5 11.6 %all-to-all-start = ((bf16[128,32,1152]{2,1,0:T(8,128)(2,1)}), bf16[128,32,1152]{2,1,0:T(8,128)(2,1)}, u32[]{:S(2)}, u32[]{:S(2)}) async-start(bf16[128,32,1152]{2,1,0:T(8,128)(2,1)} %stack.2), calls=%async_computation | async-start | bytes 18874368 | tf_op jit(solution)/shard_map/all_to_all | solution.py:11
  24.1 0.0 reduce-scatter.2.cloned.1.call-start
  25.5 113.4 %all-to-all-done = bf16[128,32,1152]{2,1,0:T(8,128)(2,1)} async-done(((bf16[128,32,1152]{2,1,0:T(8,128)(2,1)}), bf16[128,32,1152]{2,1,0:T(8,128)(2,1)}, u32[]{:S(2)}, u32[]{:S(2)}) %all-to-all-start) | async-done | bytes 9437216 | tf_op jit(solution)/shard_map/all_to_all | solution.py:11
  138.9 0.0 copy-done
  138.9 0.0 copy-done.1
  138.9 19.9 %fusion.1 = bf16[1024,4096]{1,0:T(8,128)(2,1)} fusion(bf16[1024,1152]{1,0:T(8,128)(2,1)S(1)} %copy-done, bf16[4096,1152]{1,0:T(8,128)(2,1)} %bitcast, f32[]{:T(128)S(6)} %copy.8, f32[]{:T(128)S(6)} %copy.7, s32[1024]{0:T(1024)S(1)} %copy-done.1, f32[]{:T(128)S(6)} %neg.9), kind=kOutput, calls=%fused_computation.3 | convolution fusion | flops 9714008064 | bytes 20189196 | tf_op jit(solution)/shard_map/dot_general | solution.py:13
  158.8 15.7 %convolution_convert_fusion = bf16[4096,1152]{1,0:T(8,128)(2,1)} fusion(bf16[1024,4096]{1,0:T(8,128)(2,1)} %fusion.1, bf16[1024,1152]{1,0:T(8,128)(2,1)S(1)} %copy-done), kind=kOutput, calls=%fused_computation.10 | convolution fusion | flops 9668395008 | bytes 20185088 | tf_op jit(solution)/shard_map/dot_general | solution.py:21
  174.5 0.0 reduce-scatter.2.cloned.1.call-update
  174.5 17.7 %fusion.7 = f32[1024,1152]{1,0:T(8,128)} fusion(bf16[1024,4096]{1,0:T(8,128)(2,1)} %fusion.1, bf16[4096,1152]{1,0:T(8,128)(2,1)} %bitcast), kind=kOutput, calls=%fused_computation.11 | convolution fusion | flops 9663676416 | bytes 22544384 | tf_op jit(solution)/shard_map/dot_general | solution.py:20
  192.2 201.6 %reduce-scatter.2.cloned.1.call-done = bf16[32,1152]{1,0:T(8,128)(2,1)} async-done(((bf16[4096,1152]{1,0:T(8,128)(2,1)}), bf16[32,1152]{1,0:T(8,128)(2,1)}) %reduce-scatter.2.cloned.1.call-update) | async-done | bytes 73744 | tf_op jit(solution)/shard_map/reduce_scatter | solution.py:24
  393.9 1.6 convert_element_type.11
Async XLA Ops:
  7.2 131.8 %copy-start = (bf16[1024,1152]{1,0:T(8,128)(2,1)S(1)}, bf16[1024,1152]{1,0:T(8,128)(2,1)}, u32[]{:S(2)}) copy-start(bf16[1024,1152]{1,0:T(8,128)(2,1)} %param.5) | copy-start | bytes 7077892
  12.5 126.4 %copy-start.1 = (s32[1024]{0:T(1024)S(1)}, s32[1024]{0:T(1024)}, u32[]{:S(2)}) copy-start(s32[1024]{0:T(1024)} %param.7) | copy-start | bytes 12292
  12.5 126.4 %all-to-all-start = ((bf16[128,32,1152]{2,1,0:T(8,128)(2,1)}), bf16[128,32,1152]{2,1,0:T(8,128)(2,1)}, u32[]{:S(2)}, u32[]{:S(2)}) async-start(bf16[128,32,1152]{2,1,0:T(8,128)(2,1)} %stack.2), calls=%async_computation | async-start | bytes 18874368 | tf_op jit(solution)/shard_map/all_to_all | solution.py:11
  24.1 369.7 %reduce-scatter.2.cloned.1.call-start = ((), (), s32[]{:S(2)}) async-start(), calls=%async_computation.2 | async-start | bytes 9510912 | tf_op jit(solution)/shard_map/reduce_scatter | solution.py:24
Sparse Core Ops, SparseCore 0:
  174.6 219.1 reduce-scatter.1
